TPU v7x, 32 devices: a whole 2x2x4 slice. The times are simulated.
32 devices in a mesh: prow: 8 (over z, y), pcol: 4 (over x, core).
Axes of the slice: x: 2, y: 2, z: 4, core: 2. Of those that a mesh axis runs over, the one named last changes fastest.
Arguments:
- front: float32 [8, 8, 16, 4, 128, 128], P(None, 'prow', None, 'pcol'), may hold values from -6 to 6, as said below
- child_blocks: float32 [1024, 128, 128], P(('prow', 'pcol')), may hold values from -3 to 3
- owners: int32 [1024, 1], P(('prow', 'pcol')), may hold values from 0 to 31; in each aligned block of 32 rows (0 to 31, 32 to 63, ...) at most 2 rows name the same one
- slots: int32 [1024], P(('prow', 'pcol')), may hold values from 1 to 127
- pattern: int32 [2, 64], replicated, may hold values 0 or 1
Outputs:
- factored: float32 [8, 8, 16, 4, 128, 128], P(None, 'prow', None, 'pcol')
Inputs may be any that keep to these rules, and one draw needn't show every extreme that they name: `front`: in the leading 2 * 256 rows and columns, off-diagonal entries lie within 2 / 512 in magnitude and diagonal entries within 3 to 5. `owners`: among the 32 child blocks of one device no owner is named more than 2 times; some owner is named exactly 2 times. `slots`: slot 0 never occurs.
All inputs are finite; a program needn't handle non-finite values.
Results may differ from a plain program's by a relative error of at most 0.0001.
Values sent between devices are 32-bit elements; how exact they have to be, the bound alone decides.
No kernel may reach another device: no remote copies, remote signals or barrier semaphores. Data moves between devices by JAX's collectives and lax.ppermute only.
A program may use at most 192 MiB of HBM per device.

v0:
```python
import jax
import jax.numpy as jnp
from jax import lax
from jax.sharding import PartitionSpec as P

CAP = 2


def local(front, child_blocks, owners, slots, pattern):
    grid_rows = lax.axis_size("prow")
    grid_cols = lax.axis_size("pcol")
    devices = grid_rows * grid_cols
    rank_r = lax.axis_index("prow")
    rank_c = lax.axis_index("pcol")
    brows = front.shape[0]
    bcols = front.shape[2]
    tile_size = front.shape[4]
    panel_width = 2 * tile_size
    local_blocks = front.reshape(brows * bcols, tile_size, tile_size)
    owner_ids = owners[:, 0]
    child_count = owner_ids.shape[0]
    same_owner = owner_ids[:, None] == owner_ids[None, :]
    earlier = lax.broadcasted_iota(jnp.int32, (child_count, child_count), 1) < lax.broadcasted_iota(
        jnp.int32, (child_count, child_count), 0
    )
    bucket_rank = jnp.sum((same_owner & earlier).astype(jnp.int32), axis=1)
    dest_slot = owner_ids * CAP + bucket_rank
    send_blocks = (
        jnp.zeros((devices * CAP, tile_size, tile_size), jnp.float32)
        .at[dest_slot]
        .set(child_blocks)
    )
    send_slots = jnp.zeros((devices * CAP,), jnp.int32).at[dest_slot].set(slots)
    got_blocks, got_slots = (
        lax.all_to_all(
            send_blocks.reshape(devices, CAP, tile_size, tile_size),
            ("prow", "pcol"),
            split_axis=0,
            concat_axis=0,
            tiled=True,
        ),
        lax.all_to_all(
            send_slots.reshape(devices, CAP),
            ("prow", "pcol"),
            split_axis=0,
            concat_axis=0,
            tiled=True,
        ),
    )
    local_blocks = local_blocks.at[got_slots.reshape(-1)].add(
        got_blocks.reshape(-1, tile_size, tile_size)
    )
    blocks = local_blocks.reshape(brows, bcols, tile_size, tile_size)
    glob_rows = jnp.arange(brows, dtype=jnp.int32) * grid_rows + rank_r
    glob_cols = jnp.arange(bcols, dtype=jnp.int32) * grid_cols + rank_c
    row_patterns = (pattern[0], jnp.maximum(pattern[0], pattern[1]))
    saved = []
    for panel_idx in range(2):
        first_block = 2 * panel_idx
        after_block = first_block + 2
        holds_panel = (rank_c >= first_block) & (rank_c < after_block)
        col_half = rank_c - first_block
        column = blocks[:, 0]
        left_part = jnp.where(holds_panel & (col_half == 0), column, 0.0)
        right_part = jnp.where(holds_panel & (col_half == 1), column, 0.0)
        contrib = jnp.concatenate([left_part, right_part], axis=2)
        row_pick = (jnp.arange(2, dtype=jnp.int32) == rank_r - first_block).astype(jnp.float32)
        summed_rows = lax.psum(contrib, "pcol")
        diag_part = row_pick[:, None, None] * summed_rows[0][None, :, :]
        pivot_block = lax.psum(diag_part.reshape(panel_width, panel_width), "prow")
        symmetric = jnp.tril(pivot_block) + jnp.tril(pivot_block, -1).T
        factor = jnp.linalg.cholesky(symmetric)
        flat_rows = summed_rows.reshape(brows * tile_size, panel_width)
        solved = jax.scipy.linalg.solve_triangular(factor, flat_rows.T, lower=True).T.reshape(
            brows, tile_size, panel_width
        )
        own_rows = (glob_rows >= first_block) & (glob_rows < after_block)
        factor_rows = factor.reshape(2, tile_size, panel_width)[
            jnp.clip(glob_rows - first_block, 0, 1)
        ]
        solved = jnp.where(own_rows[:, None, None], factor_rows, solved)
        chosen = row_patterns[panel_idx][glob_rows].astype(jnp.float32)
        keep_rows = jnp.where(own_rows, 1.0, jnp.where(glob_rows < first_block, 0.0, chosen))
        lower_rows = solved * keep_rows[:, None, None]
        source_rows = glob_cols // grid_rows
        held_here = glob_cols % grid_rows == rank_r
        col_part = jnp.where(held_here[:, None, None], lower_rows[source_rows], 0.0)
        lower_cols = lax.psum(col_part, "prow")
        row_mask = (glob_rows >= after_block).astype(jnp.float32)
        col_mask = (glob_cols >= after_block).astype(jnp.float32)
        update = jnp.einsum(
            "auk,bvk->abuv",
            lower_rows * row_mask[:, None, None],
            lower_cols * col_mask[:, None, None],
            precision=lax.Precision.HIGHEST,
        )
        blocks = blocks - update
        saved.append((holds_panel, col_half, lower_rows))
    result = blocks
    for holds_panel, col_half, lower_rows in saved:
        picked = jnp.where(
            col_half == 0, lower_rows[:, :, :tile_size], lower_rows[:, :, tile_size:]
        )
        new_column = jnp.where(holds_panel, picked, result[:, 0])
        result = result.at[:, 0].set(new_column)
    upper_mask = (glob_rows < 4)[:, None] & (glob_cols >= 4)[None, :]
    result = jnp.where(upper_mask[:, :, None, None], 0.0, result)
    return result.reshape(brows, 1, bcols, 1, tile_size, tile_size)


def solution(mesh):
    placed = (
        P(None, "prow", None, "pcol", None, None),
        P(("prow", "pcol"), None, None),
        P(("prow", "pcol"), None),
        P(("prow", "pcol")),
        P(),
    )
    return jax.shard_map(
        local,
        mesh=mesh,
        in_specs=placed,
        out_specs=P(None, "prow", None, "pcol", None, None),
        check_vma=False,
    )
```

profile of v0, /device:TPU:9, one launch (start us, length us, event | category | flops | bytes accessed | tf_op | source)
XLA Modules:
  0.0 770.4 jit_solution(16032242215954378485)
XLA Ops:
  6.5 7.9 %copy.153 = f32[8,1,16,1,128,128]{5,4,3,2,1,0:T(8,128)} copy(f32[8,1,16,1,128,128]{5,4,3,2,1,0:T(8,128)} %param.12) | data formatting | bytes 16777216
  16.3 6.4 all-to-all-start
  22.6 2.5 broadcast_in_dim.95
  25.1 5.4 scatter_fusion
  30.5 5.9 all-to-all-start.1
  37.8 89.9 %all-to-all-done.1 = f32[32,2,128,128]{3,2,1,0:T(8,128)} async-done(((f32[32,2,128,128]{3,2,1,0:T(8,128)}), f32[32,2,128,128]{3,2,1,0:T(8,128)}, u32[]{:S(2)}, u32[]{:S(2)}) %all-to-all-start.1) | async-done | bytes 4194336 | tf_op jit(solution)/shard_map/all_to_all | solution.py:35
  127.7 13.0 %scatter_fusion.1 = f32[128,128,128]{2,1,0:T(8,128)} fusion(f32[128,128,128]{2,1,0:T(8,128)} %bitcast.166, s32[64]{0:T(128)S(1)} %fusion.43, f32[64,128,128]{2,1,0:T(8,128)} %bitcast.7), kind=kCustom, calls=%fused_computation.8 | custom fusion | flops 1048576 | bytes 12583168 | tf_op jit(solution)/shard_map/scatter-add | solution.py:50
  140.8 9.3 %copy.87 = f32[8,16,128,128]{2,3,0,1:T(8,128)} copy(f32[8,16,128,128]{3,2,1,0:T(8,128)} %bitcast.167) | data formatting | bytes 16777216 | tf_op jit(solution)/shard_map/reshape | solution.py:53
  150.0 1.1 select_bitcast_fusion.4
  151.2 1.0 pad_maximum_fusion
  152.4 37.0 %all-reduce.8.cloned.1.call-done = f32[8,128,256]{1,2,0:T(8,128)} async-done(((f32[8,128,256]{1,2,0:T(8,128)}), f32[8,128,256]{1,2,0:T(8,128)}) %all-reduce.8.cloned.1.call-update) | async-done | bytes 1048592 | tf_op jit(solution)/shard_map/psum | solution.py:68
  192.1 1.6 copy.81
  194.0 67.9 %all-reduce.10.cloned.1.call-done = f32[256,256]{0,1:T(8,128)} async-done(((f32[256,256]{0,1:T(8,128)}), f32[256,256]{0,1:T(8,128)}) %all-reduce.10.cloned.1.call-update) | async-done | bytes 262160 | tf_op jit(solution)/shard_map/psum | solution.py:70
  261.9 1.1 copy.75
  264.3 11.7 %cholesky.130 = f32[128,128]{1,0:T(8,128)S(1)} custom-call(f32[128,128]{1,0:T(8,128)S(1)} %copy.78), custom_call_target="Cholesky" | custom-call | tf_op jit(solution)/shard_map/jit(cholesky)/cholesky | solution.py:72
  276.0 9.8 %custom-call.13 = f32[1,128,128]{1,2,0:T(8,128)S(1)} custom-call(f32[1,128,128]{2,1,0:T(8,128)S(1)} %get-tuple-element.82), custom_call_target="InvertDiagBlocksLowerTriangular" | custom-call | tf_op jit(solution)/shard_map/jit(cholesky)/cholesky | solution.py:72
  286.5 11.7 %cholesky.147 = f32[128,128]{1,0:T(8,128)S(1)} custom-call(f32[128,128]{1,0:T(8,128)S(1)} %copy.80), custom_call_target="Cholesky" | custom-call | tf_op jit(solution)/shard_map/jit(cholesky)/cholesky | solution.py:72
  300.4 4.2 while.6
  301.2 1.4 bitcast_dynamic-update-slice_fusion.5
  303.2 1.4 bitcast_dynamic-update-slice_fusion.5
  304.5 19.7 %custom-call.14 = f32[2,128,128]{1,2,0:T(8,128)S(1)} custom-call(f32[2,128,128]{2,1,0:T(8,128)S(1)} %get-tuple-element.45), custom_call_target="InvertDiagBlocksLowerTriangular" | custom-call | tf_op jit(solution)/shard_map/jit(_solve_triangular)/triangular_solve | solution.py:74
  326.7 1.3 copy.83
  328.0 1.4 fusion.4
  330.1 1.6 broadcast_select_fusion.1
  331.9 103.4 %all-reduce.12.cloned.1.call-done = f32[16,128,256]{1,2,0:T(8,128)} async-done(((f32[16,128,256]{1,2,0:T(8,128)}), f32[16,128,256]{1,2,0:T(8,128)}) %all-reduce.12.cloned.1.call-update) | async-done | bytes 2097168 | tf_op jit(solution)/shard_map/psum | solution.py:88
  435.3 11.2 %bitcast_subtract_fusion.1 = f32[8,16,128,128]{2,3,0,1:T(8,128)S(1)} fusion(f32[8,16,128,128]{2,3,0,1:T(8,128)} %copy.87, f32[16,128,256]{1,2,0:T(8,128)} %all-reduce.12.cloned.1.call-done, f32[8,128,256]{1,2,0:T(8,128)S(1)} %fusion.4, f32[16]{0:T(128)S(1)} %compare_convert_fusion.2, f32[8]{0:T(128)S(1)} %get-tuple-element.94), kind=kOutput, calls=%fused_computation.14 | convolution fusion | flops 6445334528 | bytes 19923040 | tf_op jit(solution)/shard_map/auk,bvk->abuv/dot_general | solution.py:91
  446.5 3.4 copy-done
  450.0 1.1 pad_maximum_fusion.1
  451.3 35.6 %all-reduce.14.cloned.1.call-done = f32[8,128,256]{1,2,0:T(8,128)} async-done(((f32[8,128,256]{1,2,0:T(8,128)}), f32[8,128,256]{1,2,0:T(8,128)}) %all-reduce.14.cloned.1.call-update) | async-done | bytes 1048592 | tf_op jit(solution)/shard_map/psum | solution.py:68
  490.1 1.6 copy.92
  492.0 67.3 %all-reduce.16.cloned.1.call-done = f32[256,256]{1,0:T(8,128)} async-done(((f32[256,256]{1,0:T(8,128)}), f32[256,256]{1,0:T(8,128)}) %all-reduce.16.cloned.1.call-update) | async-done | bytes 262160 | tf_op jit(solution)/shard_map/psum | solution.py:70
  561.6 11.7 %cholesky.164 = f32[128,128]{1,0:T(8,128)S(1)} custom-call(f32[128,128]{1,0:T(8,128)S(1)} %cholesky.197), custom_call_target="Cholesky" | custom-call | tf_op jit(solution)/shard_map/jit(cholesky)/cholesky | solution.py:72
  573.4 9.8 %custom-call.15 = f32[1,128,128]{1,2,0:T(8,128)S(1)} custom-call(f32[1,128,128]{2,1,0:T(8,128)S(1)} %get-tuple-element.78), custom_call_target="InvertDiagBlocksLowerTriangular" | custom-call | tf_op jit(solution)/shard_map/jit(cholesky)/cholesky | solution.py:72
  583.6 11.7 %cholesky.181 = f32[128,128]{1,0:T(8,128)S(1)} custom-call(f32[128,128]{1,0:T(8,128)S(1)} %convolution_subtract_fusion.2), custom_call_target="Cholesky" | custom-call | tf_op jit(solution)/shard_map/jit(cholesky)/cholesky | solution.py:72
  598.1 4.2 while.7
  598.9 1.3 bitcast_dynamic-update-slice_fusion.6
  601.0 1.3 bitcast_dynamic-update-slice_fusion.6
  602.3 19.7 %custom-call.16 = f32[2,128,128]{1,2,0:T(8,128)S(1)} custom-call(f32[2,128,128]{2,1,0:T(8,128)S(1)} %get-tuple-element.46), custom_call_target="InvertDiagBlocksLowerTriangular" | custom-call | tf_op jit(solution)/shard_map/jit(_solve_triangular)/triangular_solve | solution.py:74
  624.0 1.3 copy.94
  625.3 1.5 copy.96
  627.5 1.3 copy.95
  628.8 1.4 select_multiply_fusion
  630.2 2.0 gather_fusion.5
  632.2 3.1 broadcast_select_fusion
  635.5 103.4 %all-reduce.18.cloned.1.call-done = f32[16,128,256]{1,2,0:T(8,128)} async-done(((f32[16,128,256]{1,2,0:T(8,128)}), f32[16,128,256]{1,2,0:T(8,128)}) %all-reduce.18.cloned.1.call-update) | async-done | bytes 2097168 | tf_op jit(solution)/shard_map/psum | solution.py:88
  738.9 11.2 %bitcast_subtract_fusion = f32[8,16,128,128]{2,3,0,1:T(8,128)S(1)} fusion(f32[8,16,128,128]{2,3,0,1:T(8,128)} %copy-done, f32[16,128,256]{1,2,0:T(8,128)} %all-reduce.18.cloned.1.call-done, f32[8,128,256]{1,2,0:T(8,128)S(1)} %select_multiply_fusion, f32[16]{0:T(128)S(1)} %get-tuple-element.90, f32[8]{0:T(128)S(1)} %get-tuple-element.91), kind=kOutput, calls=%fused_computation.13 | convolution fusion | flops 6445334528 | bytes 19923040 | tf_op jit(solution)/shard_map/auk,bvk->abuv/dot_general | solution.py:91
  750.4 3.9 select_bitcast_fusion
  754.2 9.1 %copy.99 = f32[8,1,16,1,128,128]{5,4,3,2,1,0:T(8,128)} copy(f32[8,1,16,1,128,128]{4,5,0,2,3,1:T(8,128)} %select_bitcast_fusion) | data formatting | bytes 16777216 | tf_op jit(solution)/shard_map/reshape | solution.py:108
  (116 shorter events, 25.6 us)
Async XLA Ops:
  6.5 7.9 %copy-start.3 = (s32[32,1]{0,1:T(1,128)S(1)}, s32[32,1]{0,1:T(1,128)}, u32[]{:S(2)}) copy-start(s32[32,1]{0,1:T(1,128)} %param.14) | copy-start | bytes 388
  14.4 10.7 %copy-start.1 = (f32[32,128,128]{2,1,0:T(8,128)S(1)}, f32[32,128,128]{2,1,0:T(8,128)}, u32[]{:S(2)}) copy-start(f32[32,128,128]{2,1,0:T(8,128)} %param.13) | copy-start | bytes 6291460
  16.3 14.3 %all-to-all-start = ((s32[32,1,2]{2,1,0:T(1,128)}), s32[32,1,2]{2,1,0:T(1,128)S(1)}, u32[]{:S(2)}, u32[]{:S(2)}) async-start(s32[32,1,2]{2,1,0:T(1,128)} %bitcast.4), calls=%async_computation | async-start | bytes 32768 | tf_op jit(solution)/shard_map/all_to_all | solution.py:42
  30.5 97.2 %all-to-all-start.1 = ((f32[32,2,128,128]{3,2,1,0:T(8,128)}), f32[32,2,128,128]{3,2,1,0:T(8,128)}, u32[]{:S(2)}, u32[]{:S(2)}) async-start(f32[32,2,128,128]{3,2,1,0:T(8,128)} %bitcast.168), calls=%async_computation.1 | async-start | bytes 8388608 | tf_op jit(solution)/shard_map/all_to_all | solution.py:35
  36.4 153.0 %all-reduce.8.cloned.1.call-start = ((), (), s32[]{:S(2)}) async-start(), calls=%async_computation.2 | async-start | bytes 2097152 | tf_op jit(solution)/shard_map/psum | solution.py:68
  150.0 2.4 copy-start.2
  152.3 109.6 %all-reduce.10.cloned.1.call-start = ((), (), s32[]{:S(2)}) async-start(), calls=%async_computation.3 | async-start | bytes 524288 | tf_op jit(solution)/shard_map/psum | solution.py:70
  191.2 244.1 %all-reduce.12.cloned.1.call-start = ((), (), s32[]{:S(2)}) async-start(), calls=%async_computation.4 | async-start | bytes 4194304 | tf_op jit(solution)/shard_map/psum | solution.py:88
  331.8 155.1 %all-reduce.14.cloned.1.call-start = ((), (), s32[]{:S(2)}) async-start(), calls=%async_computation.5 | async-start | bytes 2097152 | tf_op jit(solution)/shard_map/psum | solution.py:68
  446.5 3.4 copy-start
  451.1 108.1 %all-reduce.16.cloned.1.call-start = ((), (), s32[]{:S(2)}) async-start(), calls=%async_computation.6 | async-start | bytes 524288 | tf_op jit(solution)/shard_map/psum | solution.py:70
  488.8 250.2 %all-reduce.18.cloned.1.call-start = ((), (), s32[]{:S(2)}) async-start(), calls=%async_computation.7 | async-start | bytes 4194304 | tf_op jit(solution)/shard_map/psum | solution.py:88
Sparse Core Ops, SparseCore 0:
  152.4 36.9 all-reduce.7
  193.1 68.7 all-reduce.9
  331.9 103.3 all-reduce.11
  451.3 35.5 all-reduce.13
  490.5 68.7 all-reduce.15
  635.5 103.3 all-reduce.17
where the time goes:
time: 777 us; the launch traced here: 770 us
  waiting for transfers between devices  505 us (65%)
  other arithmetic  142 us (18%)
  local copies, waits for them, and re-layouts  66.4 us (9%)
  matrix products  27.1 us (3%)
  between operations  16.8 us (2%)
  starting transfers between devices  13.1 us (2%)
    psum x2, waiting for transfers between devices, local(): lower_cols = lax.psum(col_part, 'prow')  207 us
    psum x2, waiting for transfers between devices, local(): pivot_block = lax.psum(diag_part.reshape(panel_width, panel_width), 'prow')  135 us
    all_to_all x1, waiting for transfers between devices, local(): lax.all_to_all(send_blocks.reshape(devices, CAP, tile_size, tile_size), (...  89.9 us
    psum x2, waiting for transfers between devices, local(): summed_rows = lax.psum(contrib, 'pcol')  72.6 us
    another operation x13, other arithmetic, local(): factor = jnp.linalg.cholesky(symmetric)  68.7 us
    another operation x5, other arithmetic, local(): jax.scipy.linalg.solve_triangular(factor, flat_rows.T, lower=True)  39.4 us
    dot_general x2, matrix products, local(): jnp.einsum('auk,bvk->abuv', lower_rows * row_mask[:, None, None], lower_c...  22.4 us
  transfers between devices with their start and end apart: 8, of which 7 were waited for; matrix products, arithmetic and copies ran while one was open for 2% of the time, Pallas kernels for 0%

commit v1 on v0

v1 whole, which is shorter than its diff:
```python
import functools

import jax
import jax.numpy as jnp
from jax import lax
from jax.experimental import pallas as pl
from jax.experimental.pallas import tpu as pltpu
from jax.sharding import PartitionSpec as P

ALL = ("prow", "pcol")
CHUNKS = 4
HIGHEST = lax.Precision.HIGHEST
VMEM_LIMIT = 56 * 2**20


def bits_of(size):
    return size.bit_length() - 1


def xor_send(x, axis, bit):
    size = lax.axis_size(axis)
    return lax.ppermute(x, axis, [(i, i ^ (1 << bit)) for i in range(size)])


def my_bit(axis, bit):
    return (lax.axis_index(axis) >> bit) & 1


def gather_bit(x, axis, bit):
    other = xor_send(x, axis, bit)
    low = my_bit(axis, bit) == 0
    return jnp.stack([jnp.where(low, x, other), jnp.where(low, other, x)])


def swap_bit(x, axis, bit):
    low = my_bit(axis, bit) == 0
    other = xor_send(jnp.where(low, x[1], x[0]), axis, bit)
    kept = jnp.where(low, x[0], x[1])
    return jnp.stack([jnp.where(low, kept, other), jnp.where(low, other, kept)])


def spread_high(x, axis, low_bits):
    for bit in range(low_bits, bits_of(lax.axis_size(axis))):
        other = lax.ppermute(x, axis, [(i, i | (1 << bit)) for i in range(1 << bit)])
        x = jnp.where(my_bit(axis, bit) == 1, other, x)
    return x


def nt_dot(a, b):
    return lax.dot_general(a, b, (((1,), (1,)), ((), ())), preferred_element_type=jnp.float32)


def split(x):
    high = x.astype(jnp.bfloat16)
    return high, (x - high.astype(jnp.float32)).astype(jnp.bfloat16)


def nt_dot3(a_high, a_low, b_high, b_low):
    return nt_dot(a_high, b_high) + (nt_dot(a_low, b_high) + nt_dot(a_high, b_low))


def pack_kernel(owner_ref, rank_ref, child_ref, first_ref, second_ref, sem):
    count = child_ref.shape[0]

    def to_first(k):
        return pltpu.make_async_copy(child_ref.at[k], first_ref.at[owner_ref[k]], sem.at[k])

    def to_second(k):
        return pltpu.make_async_copy(child_ref.at[k], second_ref.at[owner_ref[k]], sem.at[k])

    for k in range(count):
        pl.when(rank_ref[k] == 0)(lambda k=k: to_first(k).start())
        pl.when(rank_ref[k] != 0)(lambda k=k: to_second(k).start())
    for k in range(count):
        pl.when(rank_ref[k] == 0)(lambda k=k: to_first(k).wait())
        pl.when(rank_ref[k] != 0)(lambda k=k: to_second(k).wait())


def pack(owner_ids, rank, child_blocks, devices):
    count, tile, _ = child_blocks.shape
    shape = jax.ShapeDtypeStruct((devices, tile, tile), jnp.float32)
    return pl.pallas_call(
        pack_kernel,
        out_shape=(shape, shape),
        grid_spec=pltpu.PrefetchScalarGridSpec(
            num_scalar_prefetch=2,
            grid=(),
            in_specs=[pl.BlockSpec(memory_space=pl.ANY)],
            out_specs=(pl.BlockSpec(memory_space=pl.ANY), pl.BlockSpec(memory_space=pl.ANY)),
            scratch_shapes=[pltpu.SemaphoreType.DMA((count,))],
        ),
        name="pack_children",
    )(owner_ids, rank, child_blocks)


def strip_kernel(bcols, row_ref, strip_ref, got_ref, *rest):
    outs, (buffer, sem) = rest[:-2], rest[-2:]
    sources = got_ref.shape[0]
    brows = strip_ref.shape[0]
    depth = brows // len(outs)

    def copy(s):
        return pltpu.make_async_copy(got_ref.at[s], buffer.at[s], sem.at[s])

    for s in range(sources):
        pl.when(row_ref[s] >= 0)(lambda s=s: copy(s).start())
    for index, out in enumerate(outs):
        out[...] = strip_ref[index * depth : (index + 1) * depth]

    for s in range(sources):

        @pl.when(row_ref[s] >= 0)
        def _(s=s):
            copy(s).wait()
            for index, out in enumerate(outs):
                at = row_ref[s] - index * depth

                @pl.when((at >= 0) & (at < depth))
                def _():
                    place = jnp.clip(at, 0, depth - 1)
                    out[place] = out[place] + buffer[s]


def add_to_strip(panel_row, strip, got, bcols):
    brows, tile, _ = strip.shape
    shape = jax.ShapeDtypeStruct((brows // CHUNKS, tile, tile), jnp.float32)
    return pl.pallas_call(
        functools.partial(strip_kernel, bcols),
        out_shape=(shape,) * CHUNKS,
        grid_spec=pltpu.PrefetchScalarGridSpec(
            num_scalar_prefetch=1,
            grid=(),
            in_specs=[pl.BlockSpec(memory_space=pltpu.VMEM), pl.BlockSpec(memory_space=pl.ANY)],
            out_specs=(pl.BlockSpec(memory_space=pltpu.VMEM),) * CHUNKS,
            scratch_shapes=[
                pltpu.VMEM(got.shape, jnp.float32),
                pltpu.SemaphoreType.DMA((got.shape[0],)),
            ],
        ),
        compiler_params=pltpu.CompilerParams(vmem_limit_bytes=VMEM_LIMIT),
        name="add_panel_children",
    )(panel_row, strip, got)


def solve_rows(x, keep0, keep1, z0, a, z1):
    width = x.shape[1] // 2
    q0 = nt_dot3(*split(x[:, :width]), *z0) * keep0
    q0_parts = split(q0)
    rest = x[:, width:] - nt_dot3(*q0_parts, *a)
    q1 = nt_dot3(*split(rest), *z1) * keep1
    return q0, q1, q0_parts, split(q1)


def solve_kernel(with_panel, keep0_ref, keep1_ref, place_ref, x_ref, z_ref, high_ref, low_ref, *rest):
    n = pl.program_id(0)
    tile = x_ref.shape[-1]
    x = jnp.concatenate([x_ref[s % 2, s // 2, 0, 0] for s in range(4)], axis=1)
    factors = [(z_ref[2 * i], z_ref[2 * i + 1]) for i in range(3)]
    keep0 = keep0_ref[n].astype(jnp.float32)
    keep1 = keep1_ref[n].astype(jnp.float32)
    q0, q1, q0_parts, q1_parts = solve_rows(x, keep0, keep1, *factors)
    high_ref[...] = jnp.concatenate([q0_parts[0], q1_parts[0]], axis=1)
    low_ref[...] = jnp.concatenate([q0_parts[1], q1_parts[1]], axis=1)
    if with_panel:
        panel_ref, scratch = rest
        scratch[...] = jnp.concatenate([q0, q1], axis=1)
        panel_ref[0] = scratch[:, pl.ds(pl.multiple_of(place_ref[0] * tile, tile), tile)]


def solve(blocks, keep0, keep1, place, factors, with_panel):
    _, _, high, rows, tile, _ = blocks.shape
    count = high * rows
    width = 4 * tile
    part = jax.ShapeDtypeStruct((count * tile, width), jnp.bfloat16)
    row_spec = pl.BlockSpec((tile, width), lambda n, *_: (n, 0))
    out_shape, out_specs, scratch = [part, part], [row_spec, row_spec], []
    if with_panel:
        out_shape.append(jax.ShapeDtypeStruct((count, tile, tile), jnp.float32))
        out_specs.append(pl.BlockSpec((1, tile, tile), lambda n, *_: (n, 0, 0)))
        scratch.append(pltpu.VMEM((tile, width), jnp.float32))
    return pl.pallas_call(
        functools.partial(solve_kernel, with_panel),
        out_shape=tuple(out_shape),
        grid_spec=pltpu.PrefetchScalarGridSpec(
            num_scalar_prefetch=3,
            grid=(count,),
            in_specs=[
                pl.BlockSpec((2, 2, 1, 1, tile, tile), lambda n, *_: (0, 0, n % high, n // high, 0, 0)),
                pl.BlockSpec(factors.shape, lambda n, *_: (0, 0, 0)),
            ],
            out_specs=tuple(out_specs),
            scratch_shapes=scratch,
        ),
        compiler_params=pltpu.CompilerParams(vmem_limit_bytes=VMEM_LIMIT),
        name="solve_rows" if with_panel else "solve_columns",
    )(keep0, keep1, place, blocks, factors)


def final_kernel(bcols, panel_blocks, first_ref, second_ref, place_ref, front_ref, got1_ref, got2_ref, high_ref, low_ref,
                 panel_ref, corner_ref, *rest):
    cols, out_ref = rest[:-1], rest[-1]
    step = pl.program_id(0)
    depth = front_ref.shape[0]
    tile = front_ref.shape[-1]
    my_row, my_col, grid_rows = place_ref[0], place_ref[1], place_ref[2]
    at = 0
    for index in range(len(cols) // 2):
        col_high, col_low = cols[2 * index], cols[2 * index + 1]
        blocks = col_high.shape[0] // tile
        update = nt_dot3(high_ref[...], low_ref[...], col_high[...], col_low[...])
        for a in range(depth):
            for b in range(blocks):
                out_ref[a, 0, at + b, 0] = (
                    front_ref[a, 0, at + b, 0] - update[a * tile : (a + 1) * tile, b * tile : (b + 1) * tile]
                )
        at += blocks

    def add(slot_ref, got_ref):
        def body(s, carry):
            slot = slot_ref[s]
            a = slot // bcols - step * depth

            @pl.when((slot > 0) & (a >= 0) & (a < depth))
            def _():
                out_ref[a, 0, slot % bcols, 0] = out_ref[a, 0, slot % bcols, 0] + got_ref[s]

            return carry

        lax.fori_loop(0, got_ref.shape[0], body, 0)

    add(first_ref, got1_ref)
    add(second_ref, got2_ref)

    for a in range(depth):
        block_row = (step * depth + a) * grid_rows + my_row

        @pl.when(block_row < panel_blocks)
        def _(a=a):
            out_ref[a] = jnp.zeros(out_ref.shape[1:], jnp.float32)

        @pl.when(my_col < panel_blocks)
        def _(a=a):
            out_ref[a, 0, 0, 0] = jnp.where(block_row < panel_blocks, corner_ref[...], panel_ref[a])


def finish(first, second, place, front, got1, got2, row_high, row_low, panel, corner, cols, panel_blocks):
    brows, _, bcols, _, tile, _ = front.shape
    depth = 2
    whole = pl.BlockSpec(memory_space=pltpu.VMEM)
    big = pl.BlockSpec((depth, 1, bcols, 1, tile, tile), lambda i, *_: (i, 0, 0, 0, 0, 0))
    rows = pl.BlockSpec((depth * tile, row_high.shape[1]), lambda i, *_: (i, 0))
    return pl.pallas_call(
        functools.partial(final_kernel, bcols, panel_blocks),
        out_shape=jax.ShapeDtypeStruct(front.shape, jnp.float32),
        grid_spec=pltpu.PrefetchScalarGridSpec(
            num_scalar_prefetch=3,
            grid=(brows // depth,),
            in_specs=[big, whole, whole, rows, rows, pl.BlockSpec((depth, tile, tile), lambda i, *_: (i, 0, 0)), whole]
            + [whole] * len(cols),
            out_specs=big,
        ),
        compiler_params=pltpu.CompilerParams(vmem_limit_bytes=VMEM_LIMIT),
        name="schur_update",
    )(first, second, place, front, got1, got2, row_high, row_low, panel, corner, *cols)


def symmetric_lower(square):
    return jnp.tril(square) + jnp.tril(square, -1).T


def factor(leading, pattern, tile):
    width = leading.shape[0] // 2
    identity = jnp.eye(width, dtype=jnp.float32)

    def step(square):
        lower = jnp.linalg.cholesky(symmetric_lower(square))
        return lower, jax.scipy.linalg.solve_triangular(lower, identity, lower=True)

    l0, z0 = step(leading[:width, :width])
    keep = jnp.repeat(pattern[0, 2:4].astype(jnp.float32), tile)
    a = jnp.dot(leading[width:, :width], z0.T, precision=HIGHEST) * keep[:, None]
    l1, z1 = step(leading[width:, width:] - jnp.dot(a, a.T, precision=HIGHEST))
    return l0, a, l1, z0, z1


def local(front, child_blocks, owners, slots, pattern):
    grid_rows = lax.axis_size("prow")
    grid_cols = lax.axis_size("pcol")
    devices = grid_rows * grid_cols
    rank_r = lax.axis_index("prow")
    rank_c = lax.axis_index("pcol")
    me = rank_r * grid_cols + rank_c
    brows, _, bcols, _, tile, _ = front.shape
    row_bits, col_bits = bits_of(grid_rows), bits_of(grid_cols)
    panel_blocks = 2 * pattern.shape[0]
    panel_bits = bits_of(panel_blocks)
    owner_ids = owners[:, 0]
    children = owner_ids.shape[0]

    def ranks(owner, slot):
        panel = (slot % bcols == 0) & (owner % grid_cols < panel_blocks)
        same = owner[..., :, None] == owner[..., None, :]
        index = jnp.arange(children, dtype=jnp.int32)
        ahead = jnp.where(
            panel[..., :, None] == panel[..., None, :], index[None, :] < index[:, None], panel[..., None, :]
        )
        return jnp.sum((same & ahead).astype(jnp.int32), axis=-1), panel

    rank, _ = ranks(owner_ids, slots)
    send1, send2 = pack(owner_ids, rank, child_blocks, devices)
    got1 = lax.all_to_all(send1, ALL, 0, 0, tiled=True)

    corner = front[0, 0, 0, 0]
    corner = spread_high(corner, "prow", panel_bits)
    corner = spread_high(corner, "pcol", panel_bits)
    for bit in reversed(range(panel_bits)):
        corner = gather_bit(corner, "prow", bit)
    for bit in reversed(range(panel_bits)):
        corner = gather_bit(corner, "pcol", bit)
    leading = jnp.transpose(corner, (3, 2, 4, 1, 0, 5)).reshape(panel_blocks * tile, panel_blocks * tile)
    l0, a, l1, z0, z1 = factor(leading, pattern, tile)
    highs = [lax.reduce_precision(whole, 8, 7) for whole in (z0, a, z1)]
    lows = [whole - high for whole, high in zip((z0, a, z1), highs)]
    factors = jnp.stack([part for pair in zip(highs, lows) for part in pair]).astype(jnp.bfloat16)
    corners = jnp.concatenate(
        [jnp.concatenate([l0, jnp.zeros_like(l0)], axis=1), jnp.concatenate([a, l1], axis=1)], axis=0
    ).reshape(panel_blocks, tile, panel_blocks, tile)
    own_row = jnp.minimum(rank_r, panel_blocks - 1)
    own_col = jnp.minimum(rank_c, panel_blocks - 1)
    own_corner = corners[own_row, :, own_col, :]

    every = lax.all_gather(jnp.stack([owner_ids, slots]), ALL)
    every_owner, every_slot = every[:, 0], every[:, 1]
    every_rank, every_panel = ranks(every_owner, every_slot)
    mine = every_owner == me
    trail_slot = jnp.where(mine & ~every_panel, every_slot, 0)
    first_slots = jnp.sum(jnp.where(every_rank == 0, trail_slot, 0), axis=1)
    second_slots = jnp.sum(jnp.where(every_rank == 1, trail_slot, 0), axis=1)
    panel_row = jnp.sum(jnp.where(mine & every_panel & (every_rank == 0), every_slot // bcols + 1, 0), axis=1) - 1

    strip = front[:, 0, 0, 0]
    late = every_panel & (every_rank == 1)
    order = jnp.cumsum(late.astype(jnp.int32), axis=1)
    rounds = jnp.max(order[:, -1])

    def deliver(turn, strip):
        chosen = late & (order == turn + 1)
        block = child_blocks[jnp.argmax(chosen[me])]
        for axis, bits in (("prow", row_bits), ("pcol", col_bits)):
            for bit in reversed(range(bits)):
                block = gather_bit(block, axis, bit)
        bits = row_bits + col_bits
        blocks = jnp.transpose(block, tuple(reversed(range(bits))) + (bits, bits + 1)).reshape(devices, tile, tile)
        here = jnp.any(chosen & mine, axis=1)
        rows = jnp.sum(jnp.where(chosen & mine, every_slot // bcols, 0), axis=1)
        return strip.at[rows].add(jnp.where(here[:, None, None], blocks, 0.0))

    strip = lax.fori_loop(0, rounds, deliver, strip)

    chunks = add_to_strip(panel_row, strip, got1, bcols)
    got2 = lax.all_to_all(send2, ALL, 0, 0, tiled=True)
    keep = (pattern[0], jnp.maximum(pattern[0], pattern[1]))
    place = jnp.stack([rank_r, rank_c, jnp.int32(grid_rows)])
    high_count = grid_rows // grid_cols
    high_bits = row_bits - col_bits
    depth = brows // CHUNKS
    cols, row_parts = [], []
    for index, chunk in enumerate(chunks):
        rows = jnp.arange(index * depth, (index + 1) * depth, dtype=jnp.int32)
        chunk = spread_high(chunk, "pcol", panel_bits)
        row = chunk
        for bit in reversed(range(panel_bits)):
            row = gather_bit(row, "pcol", bit)
        row_parts.append(row)
        x = chunk
        for bit in reversed(range(row_bits)):
            x = gather_bit(x, "prow", bit)
            if bit < panel_bits:
                x = swap_bit(x, "pcol", bit)
            elif bit < col_bits:
                x = jnp.where(my_bit("pcol", bit) == 0, x[0], x[1])
        x = jnp.transpose(
            x, (0, 1) + tuple(reversed(range(2, 2 + high_bits))) + tuple(range(2 + high_bits, 5 + high_bits))
        ).reshape(2, 2, high_count, depth, tile, tile)
        blocks = (rows[:, None] * grid_rows + jnp.arange(high_count, dtype=jnp.int32) * grid_cols + rank_c).reshape(-1)
        cols += solve(x, keep[0][blocks], keep[1][blocks], rank_c[None], factors, False)
    row = jnp.concatenate(row_parts, axis=2)[:, :, None]
    blocks = jnp.arange(brows, dtype=jnp.int32) * grid_rows + rank_r
    row_high, row_low, panel = solve(row, keep[0][blocks], keep[1][blocks], own_col[None], factors, True)
    return finish(
        first_slots, second_slots, place, front, got1, got2, row_high, row_low, panel, own_corner, cols, panel_blocks
    )


def solution(mesh):
    placed = (
        P(None, "prow", None, "pcol", None, None),
        P(("prow", "pcol"), None, None),
        P(("prow", "pcol"), None),
        P(("prow", "pcol")),
        P(),
    )
    return jax.shard_map(
        local,
        mesh=mesh,
        in_specs=placed,
        out_specs=P(None, "prow", None, "pcol", None, None),
        check_vma=False,
    )
```

time: 777 us -> 610 us (0.79); the launches traced: 770 us -> 613 us
  waiting for transfers between devices: 505 us -> 122 us
  Pallas kernels: 0 us -> 123 us
  blocking collectives: 0 us -> 70.9 us
  starting transfers between devices: 13.1 us -> 74 us
  local copies, waits for them, and re-layouts: 66.4 us -> 50.1 us
  matrix products: 27.1 us -> 13.2 us
  between operations: 16.8 us -> 3.82 us
  other arithmetic: 142 us -> 153 us
    psum x6 -> x0, waiting for transfers between devices: 415 us -> none  [the longest x2 207 us: local(): lower_cols = lax.psum(col_part, 'prow')]
    pallas_call x0 -> x8, Pallas kernels: none -> 123 us  [the longest x1 65.6 us: pack(): pl.pallas_call(pack_kernel, out_shape=(shape, shape), grid_spec=pltpu.Pre...]
    ppermute x0 -> x38, waiting for transfers between devices: none -> 122 us  [the longest x37 122 us: xor_send(): return lax.ppermute(x, axis, [(i, i ^ 1 << bit) for i in range(size)])]
    all_to_all x2, waiting for transfers between devices: 89.9 us -> 0.01 us  [the longest x1 0.01 us: local(): got1 = lax.all_to_all(send1, ALL, 0, 0, tiled=True)]
    all_gather x0 -> x1, blocking collectives: none -> 70.9 us  [local(): every = lax.all_gather(jnp.stack([owner_ids, slots]), ALL)]
    ppermute x0 -> x38, starting transfers between devices: none -> 64.1 us  [the longest x37 59.9 us: xor_send(): return lax.ppermute(x, axis, [(i, i ^ 1 << bit) for i in range(size)])]
    another operation x18 -> x71, other arithmetic: 108 us -> 130 us  [the longest x13 72.3 us: step(): lower = jnp.linalg.cholesky(symmetric_lower(square))]
    dot_general x2, matrix products: 22.4 us -> 3.54 us  [the longest x1 2.17 us: factor(): l1, z1 = step(leading[width:, width:] - jnp.dot(a, a.T, precision=HIGHEST))]
  transfers between devices with their start and end apart: 8 -> 40, of which waited for: 7 -> 21; matrix products, arithmetic and copies ran while one was open for 2% -> 34% of each run, Pallas kernels for 0% -> 17%
where the time goes in v1:
time: 610 us; the launch traced here: 613 us
  other arithmetic  153 us (25%)
  Pallas kernels  123 us (20%)
  waiting for transfers between devices  122 us (20%)
  starting transfers between devices  74 us (12%)
  blocking collectives  70.9 us (12%)
  local copies, waits for them, and re-layouts  50.1 us (8%)
  matrix products  13.2 us (2%)
    ppermute x37, waiting for transfers between devices, xor_send(): return lax.ppermute(x, axis, [(i, i ^ 1 << bit) for i in range(size)])  122 us
    another operation x13, other arithmetic, step(): lower = jnp.linalg.cholesky(symmetric_lower(square))  72.3 us
    all_gather x1, blocking collectives, local(): every = lax.all_gather(jnp.stack([owner_ids, slots]), ALL)  70.9 us
    pallas_call x1, Pallas kernels, pack(): pl.pallas_call(pack_kernel, out_shape=(shape, shape), grid_spec=pltpu.Pre...  65.6 us
    ppermute x37, starting transfers between devices, xor_send(): return lax.ppermute(x, axis, [(i, i ^ 1 << bit) for i in range(size)])  59.9 us
    another operation x5, other arithmetic, step(): jax.scipy.linalg.solve_triangular(lower, identity, lower=True)  43 us
    pallas_call x5, Pallas kernels, solve(): pl.pallas_call(functools.partial(solve_kernel, with_panel), out_shape=tup...  35 us
    pallas_call x1, Pallas kernels, finish(): pl.pallas_call(functools.partial(final_kernel, bcols, panel_blocks), out_...  19.8 us
  transfers between devices with their start and end apart: 40, of which 21 were waited for; matrix products, arithmetic and copies ran while one was open for 34% of the time, Pallas kernels for 17%

profile of v1, /device:TPU:9, one launch (start us, length us, event | category | flops | bytes accessed | tf_op | source)
XLA Modules:
  0.0 613.0 jit_solution(5891230051394554864)
XLA Ops:
  0.8 4.2 collective-permute-start.13
  7.2 65.6 %pack_children.1 = (f32[32,128,128]{2,1,0:T(8,128)}, f32[32,128,128]{2,1,0:T(8,128)}) custom-call(s32[32]{0:T(128)} %bitcast.312, s32[32]{0:T(128)} %convert_reduce_fusion.1.rank_ref, f32[32,128,128]{2,1,0:T(8,128)} %child_ref.1), custom_call_target="tpu_custom_call" | custom-call | tf_op jit(solution)/shard_map/pack_children/pallas_call | solution.py:82
  72.9 4.6 all-to-all-start
  78.2 70.9 %all-gather.1 = s32[32,2,32]{2,1,0:T(2,128)S(1)} all-gather(s32[1,2,32]{2,1,0:T(2,128)S(1)} %add_bitcast_fusion), channel_id=2, replica_groups=mesh['prow'=8,'pcol'=4] {'prow','pcol'}, dimensions={0}, use_global_device_ids=true | all-gather | bytes 8448 | tf_op jit(solution)/shard_map/all_gather | solution.py:332
  154.5 3.5 collective-permute-done.14
  159.3 2.6 collective-permute-done.15
  164.4 4.0 collective-permute-done.16
  170.3 2.8 collective-permute-start.17
  190.9 3.0 reshape.283
  197.0 11.7 %cholesky.130 = f32[128,128]{1,0:T(8,128)S(1)} custom-call(f32[128,128]{1,0:T(8,128)S(1)} %copy.72), custom_call_target="Cholesky" | custom-call | tf_op jit(solution)/shard_map/jit(cholesky)/cholesky | solution.py:276
  208.8 9.8 %custom-call.13 = f32[1,128,128]{1,2,0:T(8,128)S(1)} custom-call(f32[1,128,128]{2,1,0:T(8,128)S(1)} %get-tuple-element.380), custom_call_target="InvertDiagBlocksLowerTriangular" | custom-call | tf_op jit(solution)/shard_map/jit(cholesky)/cholesky | solution.py:276
  221.0 12.1 %cholesky.147 = f32[128,128]{1,0:T(8,128)S(1)} custom-call(f32[128,128]{1,0:T(8,128)S(1)} %copy.74), custom_call_target="Cholesky" | custom-call | tf_op jit(solution)/shard_map/jit(cholesky)/cholesky | solution.py:276
  236.5 4.2 while.18
  241.2 19.7 %custom-call.14 = f32[2,128,128]{1,2,0:T(8,128)S(1)} custom-call(f32[2,128,128]{2,1,0:T(8,128)S(1)} %get-tuple-element.226), custom_call_target="InvertDiagBlocksLowerTriangular" | custom-call | tf_op jit(solution)/shard_map/jit(_solve_triangular)/triangular_solve | solution.py:277
  273.3 11.7 %cholesky.164 = f32[128,128]{1,0:T(8,128)S(1)} custom-call(f32[128,128]{1,0:T(8,128)S(1)} %cholesky.197), custom_call_target="Cholesky" | custom-call | tf_op jit(solution)/shard_map/jit(cholesky)/cholesky | solution.py:276
  285.6 10.4 %custom-call.15 = f32[1,128,128]{1,2,0:T(8,128)} custom-call(f32[1,128,128]{2,1,0:T(8,128)S(1)} %get-tuple-element.376), custom_call_target="InvertDiagBlocksLowerTriangular" | custom-call | tf_op jit(solution)/shard_map/jit(cholesky)/cholesky | solution.py:276
  299.7 12.5 %cholesky.181 = f32[128,128]{1,0:T(8,128)S(1)} custom-call(f32[128,128]{1,0:T(8,128)} %convolution_subtract_fusion.3), custom_call_target="Cholesky" | custom-call | tf_op jit(solution)/shard_map/jit(cholesky)/cholesky | solution.py:276
  320.3 7.1 %while.19 = (s32[]{:T(128)}, f32[256,256]{1,0:T(8,128)}, s32[2,2]{1,0:T(2,128)}, f32[2,128,128]{2,1,0:T(8,128)S(1)}, s32[]{:T(128)}) while((s32[]{:T(128)}, f32[256,256]{1,0:T(8,128)}, s32[2,2]{1,0:T(2,128)}, f32[2,128,128]{2,1,0:T(8,128)S(1)}, s32[]{:T(128)}) %tuple.167), condition=%wide.while_cond.clone, body=%wide.while_body.clone.sunk | while | flops 2 | bytes 131189 | solution.py:277
  327.3 20.3 %custom-call.16 = f32[2,128,128]{1,2,0:T(8,128)} custom-call(f32[2,128,128]{2,1,0:T(8,128)S(1)} %get-tuple-element.227), custom_call_target="InvertDiagBlocksLowerTriangular" | custom-call | tf_op jit(solution)/shard_map/jit(_solve_triangular)/triangular_solve | solution.py:277
  358.5 5.3 all-to-all-start.1
  363.8 84.1 %while.17 = (s32[]{:T(128)}, f32[8,128,128]{2,1,0:T(8,128)S(1)}, s32[]{:T(128)}, s32[32,32]{1,0:T(8,128)}, pred[32,32]{1,0:T(8,128)(4,1)}, /*index=5*/pred[32,32...) while((s32[]{:T(128)}, f32[8,128,128]{2,1,0:T(8,128)S(1)}, ...), condition=%wide.region_12.13_spmd, body=%wide.region_7.12_spmd.sunk | while | flops 3592466 | bytes 35023256 | solution.py:358
  371.9 40.6 %collective-permute-done = f32[128,128]{1,0:T(8,128)S(1)} collective-permute-done((f32[128,128]{1,0:T(8,128)S(1)}, f32[128,128]{1,0:T(8,128)S(1)}, u32[]{:S(2)}, u32[]{:S(2)}) %collective-permute-start) | collective-permute-done | bytes 65568 | tf_op jit(solution)/shard_map/while/body/ppermute | solution.py:22
  415.8 3.0 collective-permute-done.1
  420.0 5.3 collective-permute-done.2
  426.6 9.9 %collective-permute-done.3 = f32[2,2,2,128,128]{4,3,0,1,2:T(8,128)S(1)} collective-permute-done((f32[2,2,2,128,128]{4,3,0,1,2:T(8,128)S(1)}, f32[2,2,2,128,128]{4,3,0,1,2:T(8,128)S(1)}, u32[]{:S(2)}, u32[]{:S(2)}) %collective-permute-start.3) | collective-permute-done | bytes 524320 | tf_op jit(solution)/shard_map/while/body/ppermute | solution.py:22
  437.7 3.3 collective-permute-start.4
  444.5 2.8 scatter_fusion
  447.9 2.8 add_panel_children.1
  459.1 7.2 %collective-permute-done.18 = f32[2,128,128]{2,1,0:T(8,128)S(1)} collective-permute-done((f32[2,128,128]{2,1,0:T(8,128)}, f32[2,128,128]{2,1,0:T(8,128)S(1)}, u32[]{:S(2)}, u32[]{:S(2)}) %collective-permute-start.18) | collective-permute-done | bytes 131104 | tf_op jit(solution)/shard_map/ppermute | solution.py:22
  468.5 3.0 collective-permute-start.33
  478.8 4.2 collective-permute-done.19
  483.6 5.0 collective-permute-done.24
  489.2 5.0 collective-permute-done.29
  495.4 4.4 collective-permute-done.34
  504.8 10.3 %solve_rows.1 = (bf16[1024,512]{1,0:T(8,128)(2,1)}, bf16[1024,512]{1,0:T(8,128)(2,1)}, f32[8,128,128]{2,1,0:T(8,128)}) custom-call(s32[8]{0:T(128)} %gather_fusion, s32[8]{0:T(128)} %gather_fusion.1, s32[1]{0:T(128)} %bitcast.32.place_ref, f32[2,2,1,8,128,128]{5,4,3,2,1,0:T(8,128)} %maximum_bitcast_fusion.x_ref, bf16[6,256,256]{2,1,0:T(8,128)(2,1)} %copy-done), custom_call_target="tpu_custom_call" | custom-call | tf_op jit(solution)/shard_map/solve_rows/pallas_call | solution.py:181
  519.4 4.3 collective-permute-done.35
  527.0 5.2 collective-permute-start.22
  532.2 5.8 collective-permute-done.26
  538.2 5.2 collective-permute-start.27
  543.4 5.8 collective-permute-done.31
  549.4 5.2 collective-permute-start.32
  554.7 5.8 collective-permute-done.36
  560.7 2.9 collective-permute-start.37
  564.7 6.2 %solve_columns.4 = (bf16[512,512]{1,0:T(8,128)(2,1)}, bf16[512,512]{1,0:T(8,128)(2,1)}) custom-call(s32[4]{0:T(128)} %gather_fusion.2, s32[4]{0:T(128)} %gather_fusion.3, s32[1]{0:T(128)} %bitcast.27.place_ref, f32[2,2,2,2,128,128]{5,4,3,2,1,0:T(8,128)} %pad_maximum_fusion.5.x_ref, bf16[6,256,256]{2,1,0:T(8,128)(2,1)} %copy-done), custom_call_target="tpu_custom_call" | custom-call | tf_op jit(solution)/shard_map/solve_columns/pallas_call | solution.py:181
  572.0 6.2 %solve_columns.5 = (bf16[512,512]{1,0:T(8,128)(2,1)}, bf16[512,512]{1,0:T(8,128)(2,1)}) custom-call(s32[4]{0:T(128)} %gather_fusion.4, s32[4]{0:T(128)} %gather_fusion.5, s32[1]{0:T(128)} %bitcast.27.place_ref, f32[2,2,2,2,128,128]{5,4,3,2,1,0:T(8,128)} %pad_maximum_fusion.6.x_ref, bf16[6,256,256]{2,1,0:T(8,128)(2,1)} %copy-done), custom_call_target="tpu_custom_call" | custom-call | tf_op jit(solution)/shard_map/solve_columns/pallas_call | solution.py:181
  579.4 6.2 %solve_columns.6 = (bf16[512,512]{1,0:T(8,128)(2,1)}, bf16[512,512]{1,0:T(8,128)(2,1)}) custom-call(s32[4]{0:T(128)} %gather_fusion.6, s32[4]{0:T(128)} %gather_fusion.7, s32[1]{0:T(128)} %bitcast.27.place_ref, f32[2,2,2,2,128,128]{5,4,3,2,1,0:T(8,128)} %pad_maximum_fusion.7.x_ref, bf16[6,256,256]{2,1,0:T(8,128)(2,1)} %copy-done), custom_call_target="tpu_custom_call" | custom-call | tf_op jit(solution)/shard_map/solve_columns/pallas_call | solution.py:181
  586.7 6.2 %solve_columns.7 = (bf16[512,512]{1,0:T(8,128)(2,1)}, bf16[512,512]{1,0:T(8,128)(2,1)}) custom-call(s32[4]{0:T(128)} %gather_fusion.8, s32[4]{0:T(128)} %gather_fusion.9, s32[1]{0:T(128)} %bitcast.27.place_ref, f32[2,2,2,2,128,128]{5,4,3,2,1,0:T(8,128)} %pad_maximum_fusion.8.x_ref, bf16[6,256,256]{2,1,0:T(8,128)(2,1)} %copy-done), custom_call_target="tpu_custom_call" | custom-call | tf_op jit(solution)/shard_map/solve_columns/pallas_call | solution.py:181
  592.9 19.8 %schur_update.1 = f32[8,1,16,1,128,128]{5,4,3,2,1,0:T(8,128)} custom-call(s32[32]{0:T(128)} %get-tuple-element.386.first_ref, s32[32]{0:T(128)} %get-tuple-element.385.second_ref, s32[3]{0:T(128)} %pad_add_fusion.place_ref, f32[8,1,16,1,128,128]{5,4,3,2,1,0:T(8,128)} %front_ref.1, f32[32,128,128]{2,1,0:T(8,128)} %copy-done.1, ...), custom_call_target="tpu_custom_call" | custom-call | tf_op jit(solution)/shard_map/schur_update/pallas_call | solution.py:252
  (274 shorter events, 139.4 us)
Async XLA Ops:
  0.8 152.7 %collective-permute-start.13 = (f32[128,128]{1,0:T(8,128)S(1)}, f32[128,128]{1,0:T(8,128)S(1)}, u32[]{:S(2)}, u32[]{:S(2)}) collective-permute-start(f32[128,128]{1,0:T(8,128)S(1)} %slice_bitcast_fusion.9), channel_id=1, source_target_pairs={{0,16},{4,20},{8,24},{12,28},{1,17},{5,21},{9,25},{13,29},{2,18},{... | collective-permute-start | bytes 196616 | tf_op jit(solution)/shard_map/ppermute | solution.py:44
  72.9 284.2 %all-to-all-start = ((f32[32,128,128]{2,1,0:T(8,128)}), f32[32,128,128]{2,1,0:T(8,128)S(1)}, u32[]{:S(2)}, u32[]{:S(2)}) async-start(f32[32,128,128]{2,1,0:T(8,128)} %get-tuple-element.194), calls=%async_computation | async-start | bytes 4194304 | tf_op jit(solution)/shard_map/all_to_all | solution.py:311
  150.9 8.4 %copy-start.8 = (s32[32,32]{1,0:T(8,128)}, s32[32,32]{1,0:T(8,128)S(1)}, u32[]{:S(2)}) copy-start(s32[32,32]{1,0:T(8,128)S(1)} %reduce_window_sum.11) | copy-start | bytes 12292
  154.4 3.6 collective-permute-start.14
  158.0 3.9 collective-permute-start.15
  159.3 16.6 %copy-start.15 = (s32[256]{0:T(256)}, s32[256]{0:T(256)S(1)}, u32[]{:S(2)}) copy-start(s32[256]{0:T(256)S(1)} %iota_add_fusion) | copy-start | bytes 3076
  159.3 101.9 %copy-start.3 = (f32[256,256]{1,0:T(8,128)}, f32[256,256]{1,0:T(8,128)S(1)}, u32[]{:S(2)}) copy-start(f32[256,256]{1,0:T(8,128)S(1)} %fusion.16) | copy-start | bytes 786436
  162.0 6.4 %collective-permute-start.16 = (f32[2,2,128,128]{3,2,1,0:T(8,128)S(1)}, f32[2,2,128,128]{3,2,1,0:T(8,128)}, u32[]{:S(2)}, u32[]{:S(2)}) collective-permute-start(f32[2,2,128,128]{3,2,1,0:T(8,128)S(1)} %pad_maximum_fusion.18), channel_id=1, source_target_pairs={{0,2},{1,3},{2,0},{3,1},{4,6},{5,7},{6,4},{7,5},{8,10},{9,11},{10,... | collective-permute-start | bytes 786440 | tf_op jit(solution)/shard_map/ppermute | solution.py:22
  170.3 17.6 %collective-permute-start.17 = (f32[2,2,2,128,128]{4,3,2,1,0:T(8,128)}, f32[2,2,2,128,128]{4,3,2,1,0:T(8,128)}, u32[]{:S(2)}, u32[]{:S(2)}) collective-permute-start(f32[2,2,2,128,128]{4,3,2,1,0:T(8,128)} %pad_maximum_fusion.9), channel_id=1, source_target_pairs={{0,1},{1,0},{2,3},{3,2},{4,5},{5,4},{6,7},{7,6},{8,9},{9,8},{10,11... | collective-permute-start | bytes 1572872 | tf_op jit(solution)/shard_map/ppermute | solution.py:22
  261.2 6.7 %copy-start.10 = (pred[256,256]{1,0:T(8,128)(4,1)S(1)}, pred[256,256]{1,0:T(8,128)(4,1)}, u32[]{:S(2)}) copy-start(pred[256,256]{1,0:T(8,128)(4,1)} %copy.76) | copy-start | bytes 196612
  358.5 234.4 %all-to-all-start.1 = ((f32[32,128,128]{2,1,0:T(8,128)}), f32[32,128,128]{2,1,0:T(8,128)}, u32[]{:S(2)}, u32[]{:S(2)}) async-start(f32[32,128,128]{2,1,0:T(8,128)} %get-tuple-element.195), calls=%async_computation.1 | async-start | bytes 4194304 | tf_op jit(solution)/shard_map/all_to_all | solution.py:361
  369.8 42.7 %collective-permute-start = (f32[128,128]{1,0:T(8,128)S(1)}, f32[128,128]{1,0:T(8,128)S(1)}, u32[]{:S(2)}, u32[]{:S(2)}) collective-permute-start(f32[128,128]{1,0:T(8,128)S(1)} %dynamic-slice_bitcast_fusion.2), channel_id=1, source_target_pairs={{0,16},{4,20},{8,24},{12,28},{16,0},{20,4},{24,8},{28,12},{1,17},{... | collective-permute-start | bytes 196616 | tf_op jit(solution)/shard_map/while/body/ppermute | solution.py:22
  413.4 5.4 collective-permute-start.1
  418.9 6.4 %collective-permute-start.2 = (f32[2,2,128,128]{3,2,0,1:T(8,128)S(1)}, f32[2,2,128,128]{3,2,0,1:T(8,128)S(1)}, u32[]{:S(2)}, u32[]{:S(2)}) collective-permute-start(f32[2,2,128,128]{3,2,0,1:T(8,128)S(1)} %pad_maximum_fusion.33), channel_id=1, source_target_pairs={{0,4},{4,0},{8,12},{12,8},{16,20},{20,16},{24,28},{28,24},{1,5},{5... | collective-permute-start | bytes 786440 | tf_op jit(solution)/shard_map/while/body/ppermute | solution.py:22
  425.4 11.1 %collective-permute-start.3 = (f32[2,2,2,128,128]{4,3,0,1,2:T(8,128)S(1)}, f32[2,2,2,128,128]{4,3,0,1,2:T(8,128)S(1)}, u32[]{:S(2)}, u32[]{:S(2)}) collective-permute-start(f32[2,2,2,128,128]{4,3,0,1,2:T(8,128)S(1)} %pad_maximum_fusion.34), channel_id=1, source_target_pairs={{0,2},{1,3},{2,0},{3,1},{4,6},{5,7},{6,4},{7,5},{8,10},{9,11},{10,... | collective-permute-start | bytes 1572872 | tf_op jit(solution)/shard_map/while/body/ppermute | solution.py:22
  437.7 5.8 collective-permute-start.4
  447.9 8.7 %copy-start.5 = (f32[128,256]{1,0:T(8,128)S(1)}, f32[128,256]{1,0:T(8,128)}, u32[]{:S(2)}) copy-start(f32[128,256]{1,0:T(8,128)} %copy-done.4) | copy-start | bytes 393220
  450.7 24.4 %copy-start.12 = (f32[2,128,128]{2,1,0:T(8,128)S(1)}, f32[2,128,128]{2,1,0:T(8,128)}, u32[]{:S(2)}) copy-start(f32[2,128,128]{2,1,0:T(8,128)} %get-tuple-element.199) | copy-start | bytes 393220
  450.7 15.6 %collective-permute-start.18 = (f32[2,128,128]{2,1,0:T(8,128)}, f32[2,128,128]{2,1,0:T(8,128)S(1)}, u32[]{:S(2)}, u32[]{:S(2)}) collective-permute-start(f32[2,128,128]{2,1,0:T(8,128)} %get-tuple-element.197), channel_id=1, source_target_pairs={{0,16},{4,20},{8,24},{12,28},{16,0},{20,4},{24,8},{28,12},{1,17},{... | collective-permute-start | bytes 393224 | tf_op jit(solution)/shard_map/ppermute | solution.py:22
  453.3 15.2 %collective-permute-start.5 = (f32[2,128,128]{2,1,0:T(8,128)}, f32[2,128,128]{2,1,0:T(8,128)S(1)}, u32[]{:S(2)}, u32[]{:S(2)}) collective-permute-start(f32[2,128,128]{2,1,0:T(8,128)} %get-tuple-element.197), channel_id=1, source_target_pairs={{0,2},{1,3},{2,0},{3,1},{4,6},{5,7},{6,4},{7,5},{8,10},{9,11},{10,... | collective-permute-start | bytes 393224 | tf_op jit(solution)/shard_map/ppermute | solution.py:22
  456.7 18.5 %copy-start = (bf16[6,256,256]{2,1,0:T(8,128)(2,1)}, bf16[6,256,256]{2,1,0:T(8,128)(2,1)S(1)}, u32[]{:S(2)}) copy-start(bf16[6,256,256]{2,1,0:T(8,128)(2,1)S(1)} %fusion.18.z_ref) | copy-start | bytes 2359300
  456.7 15.8 %collective-permute-start.23 = (f32[2,128,128]{2,1,0:T(8,128)}, f32[2,128,128]{2,1,0:T(8,128)S(1)}, u32[]{:S(2)}, u32[]{:S(2)}) collective-permute-start(f32[2,128,128]{2,1,0:T(8,128)} %get-tuple-element.198), channel_id=1, source_target_pairs={{0,16},{4,20},{8,24},{12,28},{16,0},{20,4},{24,8},{28,12},{1,17},{... | collective-permute-start | bytes 393224 | tf_op jit(solution)/shard_map/ppermute | solution.py:22
  456.8 15.9 %collective-permute-start.7 = (f32[2,128,128]{2,1,0:T(8,128)}, f32[2,128,128]{2,1,0:T(8,128)S(1)}, u32[]{:S(2)}, u32[]{:S(2)}) collective-permute-start(f32[2,128,128]{2,1,0:T(8,128)} %get-tuple-element.198), channel_id=1, source_target_pairs={{0,2},{1,3},{2,0},{3,1},{4,6},{5,7},{6,4},{7,5},{8,10},{9,11},{10,... | collective-permute-start | bytes 393224 | tf_op jit(solution)/shard_map/ppermute | solution.py:22
  456.8 18.1 %collective-permute-start.28 = (f32[2,128,128]{2,1,0:T(8,128)}, f32[2,128,128]{2,1,0:T(8,128)S(1)}, u32[]{:S(2)}, u32[]{:S(2)}) collective-permute-start(f32[2,128,128]{2,1,0:T(8,128)} %get-tuple-element.199), channel_id=1, source_target_pairs={{0,16},{4,20},{8,24},{12,28},{16,0},{20,4},{24,8},{28,12},{1,17},{... | collective-permute-start | bytes 393224 | tf_op jit(solution)/shard_map/ppermute | solution.py:22
  466.3 8.7 %collective-permute-start.9 = (f32[2,128,128]{2,1,0:T(8,128)}, f32[2,128,128]{2,1,0:T(8,128)S(1)}, u32[]{:S(2)}, u32[]{:S(2)}) collective-permute-start(f32[2,128,128]{2,1,0:T(8,128)} %get-tuple-element.199), channel_id=1, source_target_pairs={{0,2},{1,3},{2,0},{3,1},{4,6},{5,7},{6,4},{7,5},{8,10},{9,11},{10,... | collective-permute-start | bytes 393224 | tf_op jit(solution)/shard_map/ppermute | solution.py:22
  468.5 7.7 %collective-permute-start.33 = (f32[2,128,128]{2,1,0:T(8,128)}, f32[2,128,128]{2,1,0:T(8,128)S(1)}, u32[]{:S(2)}, u32[]{:S(2)}) collective-permute-start(f32[2,128,128]{2,1,0:T(8,128)} %get-tuple-element.200), channel_id=1, source_target_pairs={{0,16},{4,20},{8,24},{12,28},{16,0},{20,4},{24,8},{28,12},{1,17},{... | collective-permute-start | bytes 393224 | tf_op jit(solution)/shard_map/ppermute | solution.py:22
  472.4 6.2 %copy-start.11 = (f32[2,128,128]{2,1,0:T(8,128)S(1)}, f32[2,128,128]{2,1,0:T(8,128)}, u32[]{:S(2)}) copy-start(f32[2,128,128]{2,1,0:T(8,128)} %get-tuple-element.200) | copy-start | bytes 393220
  472.5 4.7 collective-permute-start.11
  472.7 28.2 %collective-permute-start.6 = (f32[2,2,128,128]{3,2,1,0:T(8,128)S(1)}, f32[2,2,128,128]{3,2,1,0:T(8,128)S(1)}, u32[]{:S(2)}, u32[]{:S(2)}) collective-permute-start(f32[2,2,128,128]{3,2,1,0:T(8,128)S(1)} %pad_maximum_fusion.14), channel_id=1, source_target_pairs={{0,1},{1,0},{2,3},{3,2},{4,5},{5,4},{6,7},{7,6},{8,9},{9,8},{10,11... | collective-permute-start | bytes 786440 | tf_op jit(solution)/shard_map/ppermute | solution.py:22
  475.0 8.0 %collective-permute-start.19 = (f32[2,2,128,128]{3,2,1,0:T(8,128)S(1)}, f32[2,2,128,128]{3,2,1,0:T(8,128)S(1)}, u32[]{:S(2)}, u32[]{:S(2)}) collective-permute-start(f32[2,2,128,128]{3,2,1,0:T(8,128)S(1)} %pad_maximum_fusion.21), channel_id=1, source_target_pairs={{0,8},{4,12},{8,0},{12,4},{16,24},{20,28},{24,16},{28,20},{1,9},{5... | collective-permute-start | bytes 786440 | tf_op jit(solution)/shard_map/ppermute | solution.py:22
  475.1 26.5 %collective-permute-start.8 = (f32[2,2,128,128]{3,2,1,0:T(8,128)S(1)}, f32[2,2,128,128]{3,2,1,0:T(8,128)S(1)}, u32[]{:S(2)}, u32[]{:S(2)}) collective-permute-start(f32[2,2,128,128]{3,2,1,0:T(8,128)S(1)} %pad_maximum_fusion.15), channel_id=1, source_target_pairs={{0,1},{1,0},{2,3},{3,2},{4,5},{5,4},{6,7},{7,6},{8,9},{9,8},{10,11... | collective-permute-start | bytes 786440 | tf_op jit(solution)/shard_map/ppermute | solution.py:22
  476.2 12.4 %collective-permute-start.24 = (f32[2,2,128,128]{3,2,1,0:T(8,128)S(1)}, f32[2,2,128,128]{3,2,1,0:T(8,128)S(1)}, u32[]{:S(2)}, u32[]{:S(2)}) collective-permute-start(f32[2,2,128,128]{3,2,1,0:T(8,128)S(1)} %pad_maximum_fusion.22), channel_id=1, source_target_pairs={{0,8},{4,12},{8,0},{12,4},{16,24},{20,28},{24,16},{28,20},{1,9},{5... | collective-permute-start | bytes 786440 | tf_op jit(solution)/shard_map/ppermute | solution.py:22
  477.2 25.4 %collective-permute-start.10 = (f32[2,2,128,128]{3,2,1,0:T(8,128)S(1)}, f32[2,2,128,128]{3,2,1,0:T(8,128)S(1)}, u32[]{:S(2)}, u32[]{:S(2)}) collective-permute-start(f32[2,2,128,128]{3,2,1,0:T(8,128)S(1)} %pad_maximum_fusion.16), channel_id=1, source_target_pairs={{0,1},{1,0},{2,3},{3,2},{4,5},{5,4},{6,7},{7,6},{8,9},{9,8},{10,11... | collective-permute-start | bytes 786440 | tf_op jit(solution)/shard_map/ppermute | solution.py:22
  483.0 11.2 %collective-permute-start.29 = (f32[2,2,128,128]{3,2,1,0:T(8,128)S(1)}, f32[2,2,128,128]{3,2,1,0:T(8,128)S(1)}, u32[]{:S(2)}, u32[]{:S(2)}) collective-permute-start(f32[2,2,128,128]{3,2,1,0:T(8,128)S(1)} %pad_maximum_fusion.23), channel_id=1, source_target_pairs={{0,8},{4,12},{8,0},{12,4},{16,24},{20,28},{24,16},{28,20},{1,9},{5... | collective-permute-start | bytes 786440 | tf_op jit(solution)/shard_map/ppermute | solution.py:22
  488.6 11.2 %collective-permute-start.34 = (f32[2,2,128,128]{3,2,1,0:T(8,128)S(1)}, f32[2,2,128,128]{3,2,1,0:T(8,128)S(1)}, u32[]{:S(2)}, u32[]{:S(2)}) collective-permute-start(f32[2,2,128,128]{3,2,1,0:T(8,128)S(1)} %pad_maximum_fusion.24), channel_id=1, source_target_pairs={{0,8},{4,12},{8,0},{12,4},{16,24},{20,28},{24,16},{28,20},{1,9},{5... | collective-permute-start | bytes 786440 | tf_op jit(solution)/shard_map/ppermute | solution.py:22
  494.2 9.0 %collective-permute-start.12 = (f32[2,2,128,128]{3,2,1,0:T(8,128)S(1)}, f32[2,2,128,128]{3,2,1,0:T(8,128)S(1)}, u32[]{:S(2)}, u32[]{:S(2)}) collective-permute-start(f32[2,2,128,128]{3,2,1,0:T(8,128)S(1)} %pad_maximum_fusion.17), channel_id=1, source_target_pairs={{0,1},{1,0},{2,3},{3,2},{4,5},{5,4},{6,7},{7,6},{8,9},{9,8},{10,11... | collective-permute-start | bytes 786440 | tf_op jit(solution)/shard_map/ppermute | solution.py:22
  499.8 15.3 %collective-permute-start.20 = (f32[2,2,128,128]{3,2,1,0:T(8,128)S(1)}, f32[2,2,128,128]{3,2,1,0:T(8,128)S(1)}, u32[]{:S(2)}, u32[]{:S(2)}) collective-permute-start(f32[2,2,128,128]{3,2,1,0:T(8,128)S(1)} %get-tuple-element.292), channel_id=1, source_target_pairs={{0,2},{1,3},{2,0},{3,1},{4,6},{5,7},{6,4},{7,5},{8,10},{9,11},{10,... | collective-permute-start | bytes 786440 | tf_op jit(solution)/shard_map/ppermute | solution.py:22
  500.8 15.5 %collective-permute-start.25 = (f32[2,2,128,128]{3,2,1,0:T(8,128)S(1)}, f32[2,2,128,128]{3,2,1,0:T(8,128)S(1)}, u32[]{:S(2)}, u32[]{:S(2)}) collective-permute-start(f32[2,2,128,128]{3,2,1,0:T(8,128)S(1)} %get-tuple-element.286), channel_id=1, source_target_pairs={{0,2},{1,3},{2,0},{3,1},{4,6},{5,7},{6,4},{7,5},{8,10},{9,11},{10,... | collective-permute-start | bytes 786440 | tf_op jit(solution)/shard_map/ppermute | solution.py:22
  501.5 16.6 %collective-permute-start.30 = (f32[2,2,128,128]{3,2,1,0:T(8,128)S(1)}, f32[2,2,128,128]{3,2,1,0:T(8,128)S(1)}, u32[]{:S(2)}, u32[]{:S(2)}) collective-permute-start(f32[2,2,128,128]{3,2,1,0:T(8,128)S(1)} %get-tuple-element.280), channel_id=1, source_target_pairs={{0,2},{1,3},{2,0},{3,1},{4,6},{5,7},{6,4},{7,5},{8,10},{9,11},{10,... | collective-permute-start | bytes 786440 | tf_op jit(solution)/shard_map/ppermute | solution.py:22
  502.5 21.2 %collective-permute-start.35 = (f32[2,2,128,128]{3,2,1,0:T(8,128)S(1)}, f32[2,2,128,128]{3,2,1,0:T(8,128)S(1)}, u32[]{:S(2)}, u32[]{:S(2)}) collective-permute-start(f32[2,2,128,128]{3,2,1,0:T(8,128)S(1)} %get-tuple-element.274), channel_id=1, source_target_pairs={{0,2},{1,3},{2,0},{3,1},{4,6},{5,7},{6,4},{7,5},{8,10},{9,11},{10,... | collective-permute-start | bytes 786440 | tf_op jit(solution)/shard_map/ppermute | solution.py:22
  515.2 11.6 %collective-permute-start.21 = (f32[2,2,2,128,128]{4,3,2,1,0:T(8,128)S(1)}, f32[2,2,2,128,128]{4,3,2,1,0:T(8,128)S(1)}, u32[]{:S(2)}, u32[]{:S(2)}) collective-permute-start(f32[2,2,2,128,128]{4,3,2,1,0:T(8,128)S(1)} %pad_maximum_fusion.10), channel_id=1, source_target_pairs={{0,4},{4,0},{8,12},{12,8},{16,20},{20,16},{24,28},{28,24},{1,5},{5... | collective-permute-start | bytes 1572872 | tf_op jit(solution)/shard_map/ppermute | solution.py:22
  516.5 21.5 %collective-permute-start.26 = (f32[2,2,2,128,128]{4,3,2,1,0:T(8,128)S(1)}, f32[2,2,2,128,128]{4,3,2,1,0:T(8,128)S(1)}, u32[]{:S(2)}, u32[]{:S(2)}) collective-permute-start(f32[2,2,2,128,128]{4,3,2,1,0:T(8,128)S(1)} %pad_maximum_fusion.11), channel_id=1, source_target_pairs={{0,4},{4,0},{8,12},{12,8},{16,20},{20,16},{24,28},{28,24},{1,5},{5... | collective-permute-start | bytes 1572872 | tf_op jit(solution)/shard_map/ppermute | solution.py:22
  518.2 31.1 %collective-permute-start.31 = (f32[2,2,2,128,128]{4,3,2,1,0:T(8,128)S(1)}, f32[2,2,2,128,128]{4,3,2,1,0:T(8,128)S(1)}, u32[]{:S(2)}, u32[]{:S(2)}) collective-permute-start(f32[2,2,2,128,128]{4,3,2,1,0:T(8,128)S(1)} %pad_maximum_fusion.12), channel_id=1, source_target_pairs={{0,4},{4,0},{8,12},{12,8},{16,20},{20,16},{24,28},{28,24},{1,5},{5... | collective-permute-start | bytes 1572872 | tf_op jit(solution)/shard_map/ppermute | solution.py:22
  523.8 36.7 %collective-permute-start.36 = (f32[2,2,2,128,128]{4,3,2,1,0:T(8,128)S(1)}, f32[2,2,2,128,128]{4,3,2,1,0:T(8,128)S(1)}, u32[]{:S(2)}, u32[]{:S(2)}) collective-permute-start(f32[2,2,2,128,128]{4,3,2,1,0:T(8,128)S(1)} %pad_maximum_fusion.13), channel_id=1, source_target_pairs={{0,4},{4,0},{8,12},{12,8},{16,20},{20,16},{24,28},{28,24},{1,5},{5... | collective-permute-start | bytes 1572872 | tf_op jit(solution)/shard_map/ppermute | solution.py:22
  527.0 36.6 %collective-permute-start.22 = (f32[2,2,2,128,128]{4,3,2,1,0:T(8,128)S(1)}, f32[2,2,2,128,128]{4,3,2,1,0:T(8,128)S(1)}, u32[]{:S(2)}, u32[]{:S(2)}) collective-permute-start(f32[2,2,2,128,128]{4,3,2,1,0:T(8,128)S(1)} %get-tuple-element.289), channel_id=1, source_target_pairs={{0,1},{1,0},{2,3},{3,2},{4,5},{5,4},{6,7},{7,6},{8,9},{9,8},{10,11... | collective-permute-start | bytes 1572872 | tf_op jit(solution)/shard_map/ppermute | solution.py:22
  538.2 32.7 %collective-permute-start.27 = (f32[2,2,2,128,128]{4,3,2,1,0:T(8,128)S(1)}, f32[2,2,2,128,128]{4,3,2,1,0:T(8,128)S(1)}, u32[]{:S(2)}, u32[]{:S(2)}) collective-permute-start(f32[2,2,2,128,128]{4,3,2,1,0:T(8,128)S(1)} %get-tuple-element.283), channel_id=1, source_target_pairs={{0,1},{1,0},{2,3},{3,2},{4,5},{5,4},{6,7},{7,6},{8,9},{9,8},{10,11... | collective-permute-start | bytes 1572872 | tf_op jit(solution)/shard_map/ppermute | solution.py:22
  549.4 28.8 %collective-permute-start.32 = (f32[2,2,2,128,128]{4,3,2,1,0:T(8,128)S(1)}, f32[2,2,2,128,128]{4,3,2,1,0:T(8,128)S(1)}, u32[]{:S(2)}, u32[]{:S(2)}) collective-permute-start(f32[2,2,2,128,128]{4,3,2,1,0:T(8,128)S(1)} %get-tuple-element.277), channel_id=1, source_target_pairs={{0,1},{1,0},{2,3},{3,2},{4,5},{5,4},{6,7},{7,6},{8,9},{9,8},{10,11... | collective-permute-start | bytes 1572872 | tf_op jit(solution)/shard_map/ppermute | solution.py:22
  560.7 24.9 %collective-permute-start.37 = (f32[2,2,2,128,128]{4,3,2,1,0:T(8,128)S(1)}, f32[2,2,2,128,128]{4,3,2,1,0:T(8,128)S(1)}, u32[]{:S(2)}, u32[]{:S(2)}) collective-permute-start(f32[2,2,2,128,128]{4,3,2,1,0:T(8,128)S(1)} %get-tuple-element.271), channel_id=1, source_target_pairs={{0,1},{1,0},{2,3},{3,2},{4,5},{5,4},{6,7},{7,6},{8,9},{9,8},{10,11... | collective-permute-start | bytes 1572872 | tf_op jit(solution)/shard_map/ppermute | solution.py:22
  (12 other events, 25.7 us)
